TPU v7x, 32 devices: a whole 2x2x4 slice. The times are simulated.
32 devices in a mesh: groups: 2 (over y), train: 4 (over z), test: 4 (over x, core).
Axes of the slice: x: 2, y: 2, z: 4, core: 2. Of those that a mesh axis runs over, the one named last changes fastest.
Arguments:
- train_feat: bfloat16 [8192, 4096], P(('groups', 'train'), 'test'), parts along dimension 0, may hold values from -6 to 6
- test_feat: bfloat16 [2048, 4096], P(('groups', 'test'), 'train'), parts along dimension 0, may hold values from -6 to 6
- inverse_kernel: bfloat16 [4096, 4096], P('train'), may hold values from -1 to 4, as said below
Outputs:
- scores: float32 [8192, 1024], P(('groups', 'train'), 'test'), parts along dimension 0
There are 2 independent parts, one for each index of `groups`. A program takes and returns all parts, laid end to end along the dimension named above; an argument that names none is the same for every part. Nothing has to cross between parts.
Inputs may be any that keep to these rules, and one draw needn't show every extreme that they name: `inverse_kernel`: symmetric.
All inputs are finite; a program needn't handle non-finite values.
Results may differ from a plain program's by a relative error of at most 0.0029.
Values may be sent and summed in bfloat16 or wider, within the bound.
A program may use at most 64 MiB of HBM per device.

v0:
```python
import jax
import jax.numpy as jnp
from jax import lax
from jax.sharding import PartitionSpec as P


def shards(train_feat, test_feat, inverse_kernel):
    partial_value = lax.dot_general(
        inverse_kernel, test_feat, (((0,), (1,)), ((), ())), preferred_element_type=jnp.float32
    )
    precond_t = lax.psum(partial_value, "train").astype(jnp.bfloat16)
    raw = jnp.dot(
        lax.all_gather(train_feat, "test", axis=1, tiled=True),
        precond_t,
        preferred_element_type=jnp.float32,
    )
    return raw * (1.0 / precond_t.shape[0] ** 0.5)


def solution(mesh):
    placed = (P(("groups", "train"), "test"), P(("groups", "test"), "train"), P("train", None))
    return jax.shard_map(
        shards,
        mesh=mesh,
        in_specs=placed,
        out_specs=P(("groups", "train"), "test"),
        check_vma=False,
    )
```

profile of v0, /device:TPU:0, one launch (start us, length us, event | category | flops | bytes accessed | tf_op | source)
XLA Modules:
  0.0 180.1 jit_solution(14141622399600435059)
XLA Ops:
  6.5 0.0 copy-start
  6.5 0.0 all-gather.2.cloned.1.call-start
  6.5 0.7 all-gather.2.cloned.1.call-update
  7.3 0.3 copy-done
  7.6 7.8 %fusion.8 = f32[4096,256]{1,0:T(8,128)} fusion(bf16[1024,4096]{1,0:T(8,128)(2,1)} %param.5, bf16[256,1024]{1,0:T(8,128)(2,1)S(1)} %copy-done), kind=kOutput, calls=%fused_computation.4 | convolution fusion | flops 2147483648 | bytes 13107200 | tf_op jit(solution)/shard_map/dot_general | solution.py:8
  15.4 148.5 %all-reduce.1 = bf16[4096,256]{1,0:T(8,128)(2,1)S(1)} all-reduce(f32[4096,256]{1,0:T(8,128)} %fusion.8), channel_id=1, replica_groups=mesh['groups'=2,'train'=4,'test'=4] {'train'}, use_global_device_ids=true, to_apply=%region_0.0 | all-reduce | flops 1048576 | bytes 6291456 | tf_op jit(solution)/shard_map/psum | solution.py:11
  163.9 0.0 all-gather.2.cloned.1.call-done
  163.9 6.8 %fusion.5 = f32[1024,256]{0,1:T(8,128)} fusion(bf16[1024,4096]{1,0:T(8,128)(2,1)} %all-gather.2.cloned.1.call-done, bf16[4096,256]{1,0:T(8,128)(2,1)S(1)} %all-reduce.1), kind=kOutput, calls=%fused_computation.3 | convolution fusion | flops 2147745792 | bytes 11534336 | tf_op jit(solution)/shard_map/dot_general | solution.py:12
  170.7 2.5 %copy.4 = f32[1024,256]{1,0:T(8,128)} copy(f32[1024,256]{0,1:T(8,128)} %fusion.5) | data formatting | bytes 2097152 | tf_op jit(solution)/shard_map/mul | solution.py:17
Async XLA Ops:
  6.5 1.0 copy-start
  6.5 157.4 %all-gather.2.cloned.1.call-start = ((), (), s32[]{:S(2)}) async-start(), calls=%async_computation | async-start | bytes 10485760 | tf_op jit(solution)/shard_map/all_gather | solution.py:13
Sparse Core Ops, SparseCore 0:
  8.9 60.9 all-gather.1
where the time goes:
time: 180 us
  blocking collectives  148 us (82%)
  matrix products  14.6 us (8%)
  between operations  13.4 us (7%)
  local copies, waits for them, and re-layouts  2.85 us (2%)
    psum x1, blocking collectives, shards(): precond_t = lax.psum(partial_value, 'train').astype(jnp.bfloat16)  148 us
    dot_general x1, matrix products, shards(): lax.dot_general(inverse_kernel, test_feat, (((0,), (1,)), ((), ())), pref...  7.8 us
    dot_general x1, matrix products, shards(): jnp.dot(lax.all_gather(train_feat, 'test', axis=1, tiled=True), precond_t...  6.82 us
  transfers between devices with their start and end apart: 1, of which 0 were waited for; matrix products, arithmetic and copies ran while one was open for 4% of the time, Pallas kernels for 0%

commit v1 on v0

v1 whole, which is shorter than its diff:
```python
import functools

import jax
import jax.numpy as jnp
from jax import lax
from jax.experimental import pallas as pl
from jax.experimental.pallas import tpu as pltpu
from jax.sharding import PartitionSpec as P

MESH = pl.DeviceIdType.MESH
CORES = 2
LAST = (((1,), (1,)), ((), ()))


def kernel(nz, nt, chunks, train_ref, test_ref, inv_ref, out_ref,
           feats, pre, train_all, inv, acc,
           local_sem, inv_sem, z_send, z_recv, x_send, x_recv, c_send, c_recv):
    nx = nt // CORES
    z = lax.axis_index("train")
    s = lax.axis_index("test")
    x, core = s // CORES, s % CORES
    twin = {"test": x * CORES + 1 - core}
    rows, fz = test_ref.shape
    fs = train_ref.shape[1]
    part = rows // chunks
    up, down = {"train": z + 1}, {"train": z - 1}
    has_up, has_down = z < nz - 1, z > 0

    def as_int(flag):
        return jnp.where(flag, 1, 0)

    barrier = pltpu.get_barrier_semaphore()
    pl.semaphore_signal(barrier, inc=1, device_id=twin, device_id_type=MESH)
    links = 1 + as_int(has_up) + as_int(has_down) + as_int(x > 0) + as_int(x < nx - 1)

    @pl.when(has_up)
    def _():
        pl.semaphore_signal(barrier, inc=1, device_id=up, device_id_type=MESH)

    @pl.when(has_down)
    def _():
        pl.semaphore_signal(barrier, inc=1, device_id=down, device_id_type=MESH)

    @pl.when(x > 0)
    def _():
        pl.semaphore_signal(barrier, inc=1, device_id={"test": s - CORES}, device_id_type=MESH)

    @pl.when(x < nx - 1)
    def _():
        pl.semaphore_signal(barrier, inc=1, device_id={"test": s + CORES}, device_id_type=MESH)

    own_test = pltpu.make_async_copy(
        test_ref, feats.at[:, pl.ds(pl.multiple_of(z * fz, fz), fz)], local_sem.at[0])
    own_train = pltpu.make_async_copy(train_ref, train_all.at[s], local_sem.at[1])
    own_test.start()

    @pl.loop(0, nz)
    def _(j):
        pltpu.make_async_copy(
            inv_ref.at[:, pl.ds(pl.multiple_of(j * fz, fz), fz)], inv.at[j], inv_sem.at[j]).start()

    own_train.start()
    pl.semaphore_wait(barrier, links)

    def block(stream, c, j):
        buf = (feats, pre)[stream]
        return buf.at[pl.ds(c * part, part), pl.ds(pl.multiple_of(j * fz, fz), fz)]

    def z_copy(stream, c, h, way, first=False):
        j = z - h if way == 0 else z + h
        dst = block(stream, c, j)
        src = test_ref.at[pl.ds(c * part, part), :] if first and stream == 0 else dst
        return pltpu.make_async_remote_copy(
            src_ref=src, dst_ref=dst,
            send_sem=z_send.at[stream, way, c, h], recv_sem=z_recv.at[stream, way, c, h],
            device_id=up if way == 0 else down, device_id_type=MESH)

    def z_sends(h, way):
        return ((z >= h) & has_up) if way == 0 else ((z + h < nz) & has_down)

    def z_start(stream, c, h, first=False):
        for way in range(2):
            @pl.when(z_sends(h, way))
            def _():
                z_copy(stream, c, h, way, first).start()

    def z_wait_recv(stream, c, h, way):
        j = z - h if way == 0 else z + h
        dst = block(stream, c, j)
        pltpu.make_async_remote_copy(
            src_ref=dst, dst_ref=dst,
            send_sem=z_send.at[stream, way, c, h - 1], recv_sem=z_recv.at[stream, way, c, h - 1],
            device_id=down if way == 0 else up, device_id_type=MESH).wait_recv()

    def z_has(h, way):
        return (z >= h) if way == 0 else (z + h < nz)

    def x_copy(h, way):
        owner = s - CORES * h if way == 0 else s + CORES * h
        return pltpu.make_async_remote_copy(
            src_ref=train_ref if h == 0 else train_all.at[owner], dst_ref=train_all.at[owner],
            send_sem=x_send.at[way, h], recv_sem=x_recv.at[way, h],
            device_id={"test": s + CORES if way == 0 else s - CORES}, device_id_type=MESH)

    def x_has(h, way):
        return (x >= h) if way == 0 else (x + h < nx)

    def x_sends(h, way):
        return x_has(h, way) & ((x < nx - 1) if way == 0 else (x > 0))

    def x_wait_recv(h, way):
        owner = s - CORES * h if way == 0 else s + CORES * h
        pltpu.make_async_remote_copy(
            src_ref=train_all.at[owner], dst_ref=train_all.at[owner],
            send_sem=x_send.at[way, h - 1], recv_sem=x_recv.at[way, h - 1],
            device_id={"test": s - CORES if way == 0 else s + CORES}, device_id_type=MESH).wait_recv()

    def twin_copy(h, way, mine=True):
        c = core if mine else 1 - core
        owner = (x - h if way == 0 else x + h) * CORES + c
        return pltpu.make_async_remote_copy(
            src_ref=train_ref if h == 0 else train_all.at[owner], dst_ref=train_all.at[owner],
            send_sem=c_send.at[way, h], recv_sem=c_recv.at[way, h],
            device_id=twin, device_id_type=MESH)

    def precond(c, h):
        for way in range(2):
            @pl.when(z_has(h, way))
            def _():
                j = z - h if way == 0 else z + h
                acc[...] += lax.dot_general(
                    block(0, c, j)[...], inv[j], LAST, preferred_element_type=jnp.float32)

    def step(i):
        t, p = i < chunks, i >= 1
        if t:
            z_start(0, i, 0, True)
        if p:
            z_start(1, i - 1, 0)
        if i == 0:
            for way in range(2):
                @pl.when(x_sends(0, way))
                def _():
                    x_copy(0, way).start()
            twin_copy(0, 0).start()
            own_test.wait()

            @pl.loop(0, nz)
            def _(j):
                pltpu.make_async_copy(
                    inv_ref.at[:, pl.ds(pl.multiple_of(j * fz, fz), fz)], inv.at[j], inv_sem.at[j]).wait()
        if i == chunks:
            own_train.wait()
            for h in range(1, nx):
                for way in range(2):
                    @pl.when(x_has(h, way))
                    def _():
                        x_wait_recv(h, way)

                        @pl.when(x_sends(h, way))
                        def _():
                            x_copy(h, way).start()

                        twin_copy(h, way).start()
        if t:
            acc[...] = lax.dot_general(
                block(0, i, z)[...], inv[z], LAST, preferred_element_type=jnp.float32)

        @pl.loop(1, nz)
        def _(h):
            for stream, c, on in ((0, i, t), (1, i - 1, p)):
                if not on:
                    continue
                for way in range(2):
                    @pl.when(z_has(h, way))
                    def _():
                        z_wait_recv(stream, c, h, way)

                        @pl.when(z_sends(h, way))
                        def _():
                            z_copy(stream, c, h, way).start()
            if t:
                precond(i, h)

        if t:
            block(1, i, z)[...] = acc[...].astype(jnp.bfloat16)

    for i in range(chunks + 1):
        step(i)

    twin_copy(0, 0, False).wait_recv()
    for h in range(1, nx):
        for way in range(2):
            @pl.when(x_has(h, way))
            def _():
                twin_copy(h, way, False).wait_recv()

    scale = 1.0 / (fz * nz) ** 0.5
    total = jnp.zeros(out_ref.shape, jnp.float32)
    for k in range(nt):
        total += lax.dot_general(
            train_all[k], pre[:, k * fs:(k + 1) * fs], LAST, preferred_element_type=jnp.float32)
    out_ref[...] = total * scale

    twin_copy(0, 0).wait_send()
    for h in range(nx):
        for way in range(2):
            @pl.when(x_sends(h, way))
            def _():
                x_copy(h, way).wait_send()
            if h > 0:
                @pl.when(x_has(h, way))
                def _():
                    twin_copy(h, way).wait_send()
    for c in range(chunks):
        for stream in range(2):
            @pl.loop(0, nz)
            def _(h):
                for way in range(2):
                    @pl.when(z_sends(h, way))
                    def _():
                        z_copy(stream, c, h, way).wait_send()


def shards(nz, nt, train_feat, test_feat, inverse_kernel):
    chunks = 4
    rows, fz = test_feat.shape
    train_rows, fs = train_feat.shape
    d = fz * nz
    nx = nt // CORES
    dma = pltpu.SemaphoreType.DMA
    anywhere = pl.BlockSpec(memory_space=pl.ANY)
    return pl.pallas_call(
        functools.partial(kernel, nz, nt, chunks),
        out_shape=jax.ShapeDtypeStruct((train_rows, rows), jnp.float32),
        in_specs=[anywhere] * 3,
        out_specs=pl.BlockSpec(memory_space=pltpu.VMEM),
        scratch_shapes=[
            pltpu.VMEM((rows, d), jnp.bfloat16),
            pltpu.VMEM((rows, d), jnp.bfloat16),
            pltpu.VMEM((nt, train_rows, fs), jnp.bfloat16),
            pltpu.VMEM((nz, fz, fz), jnp.bfloat16),
            pltpu.VMEM((rows // chunks, fz), jnp.float32),
            dma((2,)),
            dma((nz,)),
            dma((2, 2, chunks, nz)),
            dma((2, 2, chunks, nz)),
            dma((2, nx)),
            dma((2, nx)),
            dma((2, nx)),
            dma((2, nx)),
        ],
        compiler_params=pltpu.CompilerParams(
            collective_id=0, has_side_effects=True, vmem_limit_bytes=56 * 1024 * 1024),
        cost_estimate=pl.CostEstimate(
            flops=2 * rows * d * (fz + train_rows), bytes_accessed=16 * 2 ** 20, transcendentals=0),
    )(train_feat, test_feat, inverse_kernel)


def solution(mesh):
    placed = (P(("groups", "train"), "test"), P(("groups", "test"), "train"), P("train", None))
    return jax.shard_map(
        functools.partial(shards, mesh.shape["train"], mesh.shape["test"]),
        mesh=mesh,
        in_specs=placed,
        out_specs=P(("groups", "train"), "test"),
        check_vma=False,
    )
```

time: 180 us -> 88.9 us (0.49)
  blocking collectives: 148 us -> 0 us
  Pallas kernels: 0 us -> 86.5 us
  matrix products: 14.6 us -> 0 us
  between operations: 13.4 us -> 0.01 us
    psum x1 -> x0, blocking collectives: 148 us -> none  [shards(): precond_t = lax.psum(partial_value, 'train').astype(jnp.bfloat16)]
    pallas_call x0 -> x1, Pallas kernels: none -> 86.5 us  [shards(): pl.pallas_call(functools.partial(kernel, nz, nt, chunks), out_shape=jax.S...]
    dot_general x2 -> x0, matrix products: 14.6 us -> none  [the longest x1 7.8 us: shards(): lax.dot_general(inverse_kernel, test_feat, (((0,), (1,)), ((), ())), pref...]
    mul x1 -> x0, local copies, waits for them, and re-layouts: 2.53 us -> none  [shards(): return raw * (1.0 / precond_t.shape[0] ** 0.5)]
    unnamed x2 -> x1, local copies, waits for them, and re-layouts: 0.32 us -> 2.26 us
  transfers between devices with their start and end apart: 1 -> 0, of which waited for: 0 -> 0; matrix products, arithmetic and copies ran while one was open for 4% -> 0% of each run, Pallas kernels for 0% -> 0%
where the time goes in v1:
time: 88.9 us; the launch traced here: 88.8 us
  Pallas kernels  86.5 us (97%)
  local copies, waits for them, and re-layouts  2.26 us (3%)
    pallas_call x1, Pallas kernels, shards(): pl.pallas_call(functools.partial(kernel, nz, nt, chunks), out_shape=jax.S...  86.5 us
    unnamed x1, local copies, waits for them, and re-layouts  2.26 us

profile of v1, /device:TPU:0, one launch (start us, length us, event | category | flops | bytes accessed | tf_op | source)
XLA Modules:
  0.0 88.8 jit_solution(4396086348942740356)
XLA Ops:
  0.0 86.5 %shard_map.37 = f32[1024,256]{1,0:T(8,128)} custom-call(bf16[1024,1024]{1,0:T(8,128)(2,1)} %train_ref.1, bf16[256,1024]{1,0:T(8,128)(2,1)} %test_ref.1, bf16[1024,4096]{1,0:T(8,128)(2,1)} %inv_ref.1), custom_call_target="tpu_custom_call" | custom-call | flops 4294967296 | bytes 16777216 | tf_op jit(solution)/shard_map/pallas_call | solution.py:233
  86.5 2.3 %copy.5 = f32[1024,256]{1,0:T(8,128)} copy(f32[1024,256]{1,0:T(8,128)} %shard_map.37) | data formatting | bytes 2097152

commit v2 on v1

--- a/solution.py
+++ b/solution.py
@@ -13,8 +13,8 @@
 
 
 def kernel(nz, nt, chunks, train_ref, test_ref, inv_ref, out_ref,
-           feats, pre, train_all, inv, acc,
-           local_sem, inv_sem, z_send, z_recv, x_send, x_recv, c_send, c_recv):
+           feats, pre, train_all, inv, acc, terms, sum_in, sum_out,
+           local_sem, inv_sem, z_send, z_recv, x_send, x_recv, c_send, c_recv, s_send, s_recv):
     nx = nt // CORES
     z = lax.axis_index("train")
     s = lax.axis_index("test")
@@ -23,6 +23,7 @@
     rows, fz = test_ref.shape
     fs = train_ref.shape[1]
     part = rows // chunks
+    scale = 1.0 / (fz * nz) ** 0.5
     up, down = {"train": z + 1}, {"train": z - 1}
     has_up, has_down = z < nz - 1, z > 0
 
@@ -123,71 +124,117 @@
             send_sem=c_send.at[way, h], recv_sem=c_recv.at[way, h],
             device_id=twin, device_id_type=MESH)
 
-    def precond(c, h):
+    def score(h, way):
+        j = z - h if way == 0 else z + h
+        at = j * fz
+        cols = pl.ds(pl.multiple_of(at % fs, fz), fz)
+        out_ref[...] += lax.dot_general(
+            train_all[at // fs, :, cols], pre[:, pl.ds(pl.multiple_of(at, fz), fz)], LAST,
+            preferred_element_type=jnp.float32) * scale
+
+    def sum_copy(way, k):
+        return pltpu.make_async_remote_copy(
+            src_ref=sum_out.at[way, k], dst_ref=sum_in.at[way, k],
+            send_sem=s_send.at[way, k], recv_sem=s_recv.at[way, k],
+            device_id=up if way == 0 else down, device_id_type=MESH)
+
+    def sum_sends(k, way):
+        return (nz - 1 - k > z) if way == 0 else (k < z)
+
+    def sum_gets(k, way):
+        return ((nz - 1 - k >= z) & has_down) if way == 0 else ((k <= z) & has_up)
+
+    def sum_step(k):
+        for way in range(2):
+            j = nz - 1 - k if way == 0 else k
+
+            @pl.when(sum_gets(k, way))
+            def _():
+                sum_copy(way, k).wait_recv()
+
+                @pl.when(j != z)
+                def _():
+                    sum_out[way, k] = (terms[j] + sum_in[way, k].astype(jnp.float32)).astype(jnp.bfloat16)
+
+                @pl.when(j == z)
+                def _():
+                    terms[z] += sum_in[way, k].astype(jnp.float32)
+
+            @pl.when(sum_sends(k, way))
+            def _():
+                @pl.when(jnp.logical_not(sum_gets(k, way)))
+                def _():
+                    sum_out[way, k] = terms[j].astype(jnp.bfloat16)
+
+                sum_copy(way, k).start()
+
+    def z_pass(stream, c, h):
+        for way in range(2):
+            @pl.when(z_has(h, way))
+            def _():
+                z_wait_recv(stream, c, h, way)
+
+                @pl.when(z_sends(h, way))
+                def _():
+                    z_copy(stream, c, h, way).start()
+
+    z_start(0, 0, 0, True)
+    for way in range(2):
+        @pl.when(x_sends(0, way))
+        def _():
+            x_copy(0, way).start()
+    twin_copy(0, 0).start()
+    own_test.wait()
+
+    @pl.loop(0, nz)
+    def _(j):
+        pltpu.make_async_copy(
+            inv_ref.at[:, pl.ds(pl.multiple_of(j * fz, fz), fz)], inv.at[j], inv_sem.at[j]).wait()
+
+    def term(j):
+        terms[j] = jnp.dot(block(0, 1, z)[...], inv[j], preferred_element_type=jnp.float32)
+
+    @pl.loop(0, nz)
+    def _(k):
+        term(jnp.where(k % 2 == 0, nz - 1 - k // 2, k // 2))
+
+    sum_step(0)
+    acc[...] = lax.dot_general(
+        block(0, 0, z)[...], inv[z], LAST, preferred_element_type=jnp.float32)
+
+    @pl.loop(1, nz)
+    def _(h):
+        z_pass(0, 0, h)
+        sum_step(h)
         for way in range(2):
             @pl.when(z_has(h, way))
             def _():
                 j = z - h if way == 0 else z + h
                 acc[...] += lax.dot_general(
-                    block(0, c, j)[...], inv[j], LAST, preferred_element_type=jnp.float32)
-
-    def step(i):
-        t, p = i < chunks, i >= 1
-        if t:
-            z_start(0, i, 0, True)
-        if p:
-            z_start(1, i - 1, 0)
-        if i == 0:
-            for way in range(2):
-                @pl.when(x_sends(0, way))
-                def _():
-                    x_copy(0, way).start()
-            twin_copy(0, 0).start()
-            own_test.wait()
-
-            @pl.loop(0, nz)
-            def _(j):
-                pltpu.make_async_copy(
-                    inv_ref.at[:, pl.ds(pl.multiple_of(j * fz, fz), fz)], inv.at[j], inv_sem.at[j]).wait()
-        if i == chunks:
-            own_train.wait()
-            for h in range(1, nx):
-                for way in range(2):
-                    @pl.when(x_has(h, way))
-                    def _():
-                        x_wait_recv(h, way)
-
-                        @pl.when(x_sends(h, way))
-                        def _():
-                            x_copy(h, way).start()
-
-                        twin_copy(h, way).start()
-        if t:
-            acc[...] = lax.dot_general(
-                block(0, i, z)[...], inv[z], LAST, preferred_element_type=jnp.float32)
-
-        @pl.loop(1, nz)
-        def _(h):
-            for stream, c, on in ((0, i, t), (1, i - 1, p)):
-                if not on:
-                    continue
-                for way in range(2):
-                    @pl.when(z_has(h, way))
-                    def _():
-                        z_wait_recv(stream, c, h, way)
-
-                        @pl.when(z_sends(h, way))
-                        def _():
-                            z_copy(stream, c, h, way).start()
-            if t:
-                precond(i, h)
-
-        if t:
-            block(1, i, z)[...] = acc[...].astype(jnp.bfloat16)
-
-    for i in range(chunks + 1):
-        step(i)
-
+                    block(0, 0, j)[...], inv[j], LAST, preferred_element_type=jnp.float32)
+
+    block(1, 0, z)[...] = acc[...].astype(jnp.bfloat16)
+    z_start(1, 0, 0)
+    block(1, 1, z)[...] = terms[z].astype(jnp.bfloat16)
+    z_start(1, 1, 0)
+
+    @pl.loop(1, nz - 1)
+    def _(h):
+        z_pass(1, 0, h)
+        z_pass(1, 1, h)
+
+    own_train.wait()
+    for h in range(1, nx):
+        for way in range(2):
+            @pl.when(x_has(h, way))
+            def _():
+                x_wait_recv(h, way)
+
+                @pl.when(x_sends(h, way))
+                def _():
+                    x_copy(h, way).start()
+
+                twin_copy(h, way).start()
     twin_copy(0, 0, False).wait_recv()
     for h in range(1, nx):
         for way in range(2):
@@ -195,12 +242,22 @@
             def _():
                 twin_copy(h, way, False).wait_recv()
 
-    scale = 1.0 / (fz * nz) ** 0.5
-    total = jnp.zeros(out_ref.shape, jnp.float32)
-    for k in range(nt):
-        total += lax.dot_general(
-            train_all[k], pre[:, k * fs:(k + 1) * fs], LAST, preferred_element_type=jnp.float32)
-    out_ref[...] = total * scale
+    out_ref[...] = jnp.zeros(out_ref.shape, jnp.float32)
+    score(0, 0)
+
+    @pl.loop(1, nz - 1)
+    def _(h):
+        for way in range(2):
+            @pl.when(z_has(h, way))
+            def _():
+                score(h, way)
+
+    z_pass(1, 0, nz - 1)
+    z_pass(1, 1, nz - 1)
+    for way in range(2):
+        @pl.when(z_has(nz - 1, way))
+        def _():
+            score(nz - 1, way)
 
     twin_copy(0, 0).wait_send()
     for h in range(nx):
@@ -212,18 +269,22 @@
                 @pl.when(x_has(h, way))
                 def _():
                     twin_copy(h, way).wait_send()
-    for c in range(chunks):
-        for stream in range(2):
-            @pl.loop(0, nz)
-            def _(h):
-                for way in range(2):
-                    @pl.when(z_sends(h, way))
-                    def _():
-                        z_copy(stream, c, h, way).wait_send()
+
+    @pl.loop(0, nz)
+    def _(h):
+        for way in range(2):
+            for stream, c in ((0, 0), (1, 0), (1, 1)):
+                @pl.when(z_sends(h, way))
+                def _():
+                    z_copy(stream, c, h, way).wait_send()
+
+            @pl.when(sum_sends(h, way))
+            def _():
+                sum_copy(way, h).wait_send()
 
 
 def shards(nz, nt, train_feat, test_feat, inverse_kernel):
-    chunks = 4
+    chunks = 2
     rows, fz = test_feat.shape
     train_rows, fs = train_feat.shape
     d = fz * nz
@@ -241,6 +302,9 @@
             pltpu.VMEM((nt, train_rows, fs), jnp.bfloat16),
             pltpu.VMEM((nz, fz, fz), jnp.bfloat16),
             pltpu.VMEM((rows // chunks, fz), jnp.float32),
+            pltpu.VMEM((nz, rows // chunks, fz), jnp.float32),
+            pltpu.VMEM((2, nz, rows // chunks, fz), jnp.bfloat16),
+            pltpu.VMEM((2, nz, rows // chunks, fz), jnp.bfloat16),
             dma((2,)),
             dma((nz,)),
             dma((2, 2, chunks, nz)),
@@ -249,6 +313,8 @@
             dma((2, nx)),
             dma((2, nx)),
             dma((2, nx)),
+            dma((2, nz)),
+            dma((2, nz)),
         ],
         compiler_params=pltpu.CompilerParams(
             collective_id=0, has_side_effects=True, vmem_limit_bytes=56 * 1024 * 1024),

time: 88.9 us -> 105 us (1.18)
  Pallas kernels: 86.5 us -> 102 us
    pallas_call x1, Pallas kernels: 86.5 us -> 102 us  [shards(): pl.pallas_call(functools.partial(kernel, nz, nt, chunks), out_shape=jax.S...]
where the time goes in v2:
time: 105 us; the launch traced here: 104 us
  Pallas kernels  102 us (97%)
  local copies, waits for them, and re-layouts  2.26 us (2%)
    pallas_call x1, Pallas kernels, shards(): pl.pallas_call(functools.partial(kernel, nz, nt, chunks), out_shape=jax.S...  102 us
    unnamed x1, local copies, waits for them, and re-layouts  2.26 us

profile of v2, /device:TPU:0, one launch (start us, length us, event | category | flops | bytes accessed | tf_op | source)
XLA Modules:
  0.0 104.4 jit_solution(705158376257475251)
XLA Ops:
  0.0 102.2 %shard_map.37 = f32[1024,256]{1,0:T(8,128)} custom-call(bf16[1024,1024]{1,0:T(8,128)(2,1)} %train_ref.1, bf16[256,1024]{1,0:T(8,128)(2,1)} %test_ref.1, bf16[1024,4096]{1,0:T(8,128)(2,1)} %inv_ref.1), custom_call_target="tpu_custom_call" | custom-call | flops 4294967296 | bytes 16777216 | tf_op jit(solution)/shard_map/pallas_call | solution.py:294
  102.2 2.3 %copy.5 = f32[1024,256]{1,0:T(8,128)} copy(f32[1024,256]{1,0:T(8,128)} %shard_map.37) | data formatting | bytes 2097152

commit v3 on v2

--- a/solution.py
+++ b/solution.py
@@ -144,11 +144,12 @@
     def sum_gets(k, way):
         return ((nz - 1 - k >= z) & has_down) if way == 0 else ((k <= z) & has_up)
 
-    def sum_step(k):
-        for way in range(2):
+    def sum_step(at):
+        for way in range(2):
+            k = at - z if way == 0 else at - (nz - 1 - z)
             j = nz - 1 - k if way == 0 else k
 
-            @pl.when(sum_gets(k, way))
+            @pl.when((k >= 0) & sum_gets(k, way))
             def _():
                 sum_copy(way, k).wait_recv()
 
@@ -160,7 +161,7 @@
                 def _():
                     terms[z] += sum_in[way, k].astype(jnp.float32)
 
-            @pl.when(sum_sends(k, way))
+            @pl.when((k >= 0) & sum_sends(k, way))
             def _():
                 @pl.when(jnp.logical_not(sum_gets(k, way)))
                 def _():
@@ -202,19 +203,25 @@
     acc[...] = lax.dot_general(
         block(0, 0, z)[...], inv[z], LAST, preferred_element_type=jnp.float32)
 
-    @pl.loop(1, nz)
+    def precond(h):
+        for way in range(2):
+            @pl.when(z_has(h, way))
+            def _():
+                j = z - h if way == 0 else z + h
+                acc[...] += lax.dot_general(
+                    block(0, 0, j)[...], inv[j], LAST, preferred_element_type=jnp.float32)
+
+    @pl.loop(1, nz - 1)
     def _(h):
         z_pass(0, 0, h)
         sum_step(h)
-        for way in range(2):
-            @pl.when(z_has(h, way))
-            def _():
-                j = z - h if way == 0 else z + h
-                acc[...] += lax.dot_general(
-                    block(0, 0, j)[...], inv[j], LAST, preferred_element_type=jnp.float32)
-
+        precond(h)
+
+    z_pass(0, 0, nz - 1)
+    precond(nz - 1)
     block(1, 0, z)[...] = acc[...].astype(jnp.bfloat16)
     z_start(1, 0, 0)
+    sum_step(nz - 1)
     block(1, 1, z)[...] = terms[z].astype(jnp.bfloat16)
     z_start(1, 1, 0)
 

time: 105 us -> 68.6 us (0.65)
  Pallas kernels: 102 us -> 66.2 us
    pallas_call x1, Pallas kernels: 102 us -> 66.2 us  [shards(): pl.pallas_call(functools.partial(kernel, nz, nt, chunks), out_shape=jax.S...]
where the time goes in v3:
time: 68.6 us; the launch traced here: 68.4 us
  Pallas kernels  66.2 us (97%)
  local copies, waits for them, and re-layouts  2.26 us (3%)
    pallas_call x1, Pallas kernels, shards(): pl.pallas_call(functools.partial(kernel, nz, nt, chunks), out_shape=jax.S...  66.2 us
    unnamed x1, local copies, waits for them, and re-layouts  2.26 us

profile of v3, /device:TPU:0, one launch (start us, length us, event | category | flops | bytes accessed | tf_op | source)
XLA Modules:
  0.0 68.4 jit_solution(10953705997808186619)
XLA Ops:
  0.0 66.2 %shard_map.37 = f32[1024,256]{1,0:T(8,128)} custom-call(bf16[1024,1024]{1,0:T(8,128)(2,1)} %train_ref.1, bf16[256,1024]{1,0:T(8,128)(2,1)} %test_ref.1, bf16[1024,4096]{1,0:T(8,128)(2,1)} %inv_ref.1), custom_call_target="tpu_custom_call" | custom-call | flops 4294967296 | bytes 16777216 | tf_op jit(solution)/shard_map/pallas_call | solution.py:301
  66.2 2.3 %copy.5 = f32[1024,256]{1,0:T(8,128)} copy(f32[1024,256]{1,0:T(8,128)} %shard_map.37) | data formatting | bytes 2097152

commit v4 on v3

--- a/solution.py
+++ b/solution.py
@@ -249,8 +249,10 @@
             def _():
                 twin_copy(h, way, False).wait_recv()
 
-    out_ref[...] = jnp.zeros(out_ref.shape, jnp.float32)
-    score(0, 0)
+    own = pl.ds(pl.multiple_of((z * fz) % fs, fz), fz)
+    out_ref[...] = lax.dot_general(
+        train_all[(z * fz) // fs, :, own], pre[:, pl.ds(pl.multiple_of(z * fz, fz), fz)], LAST,
+        preferred_element_type=jnp.float32) * scale
 
     @pl.loop(1, nz - 1)
     def _(h):
@@ -259,12 +261,16 @@
             def _():
                 score(h, way)
 
-    z_pass(1, 0, nz - 1)
-    z_pass(1, 1, nz - 1)
-    for way in range(2):
-        @pl.when(z_has(nz - 1, way))
-        def _():
-            score(nz - 1, way)
+    for c in range(chunks):
+        z_pass(1, c, nz - 1)
+        for way in range(2):
+            @pl.when(z_has(nz - 1, way))
+            def _():
+                j = z - (nz - 1) if way == 0 else z + nz - 1
+                cols = pl.ds(pl.multiple_of((j * fz) % fs, fz), fz)
+                out_ref[:, c * part:(c + 1) * part] += lax.dot_general(
+                    train_all[(j * fz) // fs, :, cols], block(1, c, j)[...], LAST,
+                    preferred_element_type=jnp.float32) * scale
 
     twin_copy(0, 0).wait_send()
     for h in range(nx):

time: 68.6 us -> 68.5 us (level)
  no operation moved by 1% of the time
where the time goes in v4:
time: 68.5 us; the launch traced here: 68.4 us
  Pallas kernels  66.1 us (96%)
  local copies, waits for them, and re-layouts  2.26 us (3%)
    pallas_call x1, Pallas kernels, shards(): pl.pallas_call(functools.partial(kernel, nz, nt, chunks), out_shape=jax.S...  66.1 us
    unnamed x1, local copies, waits for them, and re-layouts  2.26 us

profile of v4, /device:TPU:0, one launch (start us, length us, event | category | flops | bytes accessed | tf_op | source)
XLA Modules:
  0.0 68.4 jit_solution(8891861550702184932)
XLA Ops:
  0.0 66.1 %shard_map.37 = f32[1024,256]{1,0:T(8,128)} custom-call(bf16[1024,1024]{1,0:T(8,128)(2,1)} %train_ref.1, bf16[256,1024]{1,0:T(8,128)(2,1)} %test_ref.1, bf16[1024,4096]{1,0:T(8,128)(2,1)} %inv_ref.1), custom_call_target="tpu_custom_call" | custom-call | flops 4294967296 | bytes 16777216 | tf_op jit(solution)/shard_map/pallas_call | solution.py:307
  66.1 2.3 %copy.5 = f32[1024,256]{1,0:T(8,128)} copy(f32[1024,256]{1,0:T(8,128)} %shard_map.37) | data formatting | bytes 2097152

commit v5 on v3

--- a/solution.py
+++ b/solution.py
@@ -22,7 +22,7 @@
     twin = {"test": x * CORES + 1 - core}
     rows, fz = test_ref.shape
     fs = train_ref.shape[1]
-    part = rows // chunks
+    first = acc.shape[0]
     scale = 1.0 / (fz * nz) ** 0.5
     up, down = {"train": z + 1}, {"train": z - 1}
     has_up, has_down = z < nz - 1, z > 0
@@ -65,12 +65,13 @@
 
     def block(stream, c, j):
         buf = (feats, pre)[stream]
-        return buf.at[pl.ds(c * part, part), pl.ds(pl.multiple_of(j * fz, fz), fz)]
-
-    def z_copy(stream, c, h, way, first=False):
+        at = pl.ds(0, first) if c == 0 else pl.ds(first, rows - first)
+        return buf.at[at, pl.ds(pl.multiple_of(j * fz, fz), fz)]
+
+    def z_copy(stream, c, h, way, fresh=False):
         j = z - h if way == 0 else z + h
         dst = block(stream, c, j)
-        src = test_ref.at[pl.ds(c * part, part), :] if first and stream == 0 else dst
+        src = test_ref.at[pl.ds(0, first), :] if fresh and stream == 0 else dst
         return pltpu.make_async_remote_copy(
             src_ref=src, dst_ref=dst,
             send_sem=z_send.at[stream, way, c, h], recv_sem=z_recv.at[stream, way, c, h],
@@ -79,11 +80,11 @@
     def z_sends(h, way):
         return ((z >= h) & has_up) if way == 0 else ((z + h < nz) & has_down)
 
-    def z_start(stream, c, h, first=False):
+    def z_start(stream, c, h, fresh=False):
         for way in range(2):
             @pl.when(z_sends(h, way))
             def _():
-                z_copy(stream, c, h, way, first).start()
+                z_copy(stream, c, h, way, fresh).start()
 
     def z_wait_recv(stream, c, h, way):
         j = z - h if way == 0 else z + h
@@ -161,12 +162,17 @@
                 def _():
                     terms[z] += sum_in[way, k].astype(jnp.float32)
 
-            @pl.when((k >= 0) & sum_sends(k, way))
-            def _():
-                @pl.when(jnp.logical_not(sum_gets(k, way)))
-                def _():
-                    sum_out[way, k] = terms[j].astype(jnp.bfloat16)
-
+            @pl.when((k >= 0) & sum_sends(k, way) & (has_down if way == 0 else has_up))
+            def _():
+                sum_copy(way, k).start()
+
+    def sum_source(k):
+        for way in range(2):
+            j = nz - 1 - k if way == 0 else k
+
+            @pl.when(jnp.logical_not(has_down if way == 0 else has_up) & (k < nz - 1))
+            def _():
+                sum_out[way, k] = terms[j].astype(jnp.bfloat16)
                 sum_copy(way, k).start()
 
     def z_pass(stream, c, h):
@@ -199,7 +205,9 @@
     def _(k):
         term(jnp.where(k % 2 == 0, nz - 1 - k // 2, k // 2))
 
-    sum_step(0)
+    ahead = 1
+    for k in range(min(ahead + 1, nz - 1)):
+        sum_source(k)
     acc[...] = lax.dot_general(
         block(0, 0, z)[...], inv[z], LAST, preferred_element_type=jnp.float32)
 
@@ -211,16 +219,36 @@
                 acc[...] += lax.dot_general(
                     block(0, 0, j)[...], inv[j], LAST, preferred_element_type=jnp.float32)
 
+    def gather_first():
+        block(1, 0, z)[...] = acc[...].astype(jnp.bfloat16)
+        z_start(1, 0, 0)
+
     @pl.loop(1, nz - 1)
     def _(h):
         z_pass(0, 0, h)
-        sum_step(h)
+        sum_source(h + ahead)
+
+        @pl.when(h < nz - 2)
+        def _():
+            sum_step(h)
+
         precond(h)
 
+    inside = has_up & has_down
+
+    @pl.when(inside)
+    def _():
+        gather_first()
+
+    if nz > 2:
+        sum_step(nz - 2)
     z_pass(0, 0, nz - 1)
-    precond(nz - 1)
-    block(1, 0, z)[...] = acc[...].astype(jnp.bfloat16)
-    z_start(1, 0, 0)
+
+    @pl.when(jnp.logical_not(inside))
+    def _():
+        precond(nz - 1)
+        gather_first()
+
     sum_step(nz - 1)
     block(1, 1, z)[...] = terms[z].astype(jnp.bfloat16)
     z_start(1, 1, 0)
@@ -293,6 +321,7 @@
 def shards(nz, nt, train_feat, test_feat, inverse_kernel):
     chunks = 2
     rows, fz = test_feat.shape
+    first = rows * 8 // 16 // 16 * 16
     train_rows, fs = train_feat.shape
     d = fz * nz
     nx = nt // CORES
@@ -308,10 +337,10 @@
             pltpu.VMEM((rows, d), jnp.bfloat16),
             pltpu.VMEM((nt, train_rows, fs), jnp.bfloat16),
             pltpu.VMEM((nz, fz, fz), jnp.bfloat16),
-            pltpu.VMEM((rows // chunks, fz), jnp.float32),
-            pltpu.VMEM((nz, rows // chunks, fz), jnp.float32),
-            pltpu.VMEM((2, nz, rows // chunks, fz), jnp.bfloat16),
-            pltpu.VMEM((2, nz, rows // chunks, fz), jnp.bfloat16),
+            pltpu.VMEM((first, fz), jnp.float32),
+            pltpu.VMEM((nz, rows - first, fz), jnp.float32),
+            pltpu.VMEM((2, nz, rows - first, fz), jnp.bfloat16),
+            pltpu.VMEM((2, nz, rows - first, fz), jnp.bfloat16),
             dma((2,)),
             dma((nz,)),
             dma((2, 2, chunks, nz)),

time: 68.6 us -> 68.5 us (level)
  no operation moved by 1% of the time
where the time goes in v5:
time: 68.5 us; the launch traced here: 68.4 us
  Pallas kernels  66.1 us (96%)
  local copies, waits for them, and re-layouts  2.26 us (3%)
    pallas_call x1, Pallas kernels, shards(): pl.pallas_call(functools.partial(kernel, nz, nt, chunks), out_shape=jax.S...  66.1 us
    unnamed x1, local copies, waits for them, and re-layouts  2.26 us

profile of v5, /device:TPU:0, one launch (start us, length us, event | category | flops | bytes accessed | tf_op | source)
XLA Modules:
  0.0 68.4 jit_solution(14448436917464677706)
XLA Ops:
  0.0 66.1 %shard_map.37 = f32[1024,256]{1,0:T(8,128)} custom-call(bf16[1024,1024]{1,0:T(8,128)(2,1)} %train_ref.1, bf16[256,1024]{1,0:T(8,128)(2,1)} %test_ref.1, bf16[1024,4096]{1,0:T(8,128)(2,1)} %inv_ref.1), custom_call_target="tpu_custom_call" | custom-call | flops 4294967296 | bytes 16777216 | tf_op jit(solution)/shard_map/pallas_call | solution.py:330
  66.1 2.3 %copy.5 = f32[1024,256]{1,0:T(8,128)} copy(f32[1024,256]{1,0:T(8,128)} %shard_map.37) | data formatting | bytes 2097152
